TPU v7x, 32 devices: a whole 2x2x4 slice. The times are simulated.
32 devices in a mesh: groups: 2 (over y), patch: 4 (over z), band: 2 (over x), width: 2 (over core).
Axes of the slice: x: 2, y: 2, z: 4, core: 2. Of those that a mesh axis runs over, the one named last changes fastest.
Arguments:
- grid_latent: bfloat16 [8192, 384], P(('groups', 'patch', 'band', 'width')), parts along dimension 0, may hold values from -6 to 6
- mesh_latent: bfloat16 [64, 32, 384], P(('groups', 'patch'), ('band', 'width')), parts along dimension 0, may hold values from -6 to 6
- w_first: bfloat16 [5, 768, 384], P(None, None, 'width'), may hold values from -0.21875 to 0.21875
- first_bias: float32 [5, 384], replicated, may hold values from -4 to 4
- w_second: bfloat16 [5, 384, 384], P(None, None, 'width'), may hold values from -0.3125 to 0.3125
- norm_gain: float32 [5, 384], replicated, may hold values from 0.5 to 1.5
- encode_source: int32 [4, 4, 512], P('patch', ('band', 'width')), may hold values from 0 to 255, as said below
- encode_target: int32 [4, 4, 512], P('patch', ('band', 'width')), may hold values from 100 to 475, as said below
- encode_count: int32 [4, 4], P('patch', ('band', 'width')), may hold values from 256 to 512
- mesh_sender: int32 [4, 4, 512], P('patch', ('band', 'width')), may hold values from 0 to 575, as said below
- mesh_receiver: int32 [4, 4, 512], P('patch', ('band', 'width')), may hold values from 0 to 63
- decode_source: int32 [4, 4, 256, 3], P('patch', ('band', 'width')), may hold values from 175 to 400, as said below
Outputs:
- grid_out: bfloat16 [8192, 384], P(('groups', 'patch', 'band', 'width')), parts along dimension 0
- mesh_out: bfloat16 [64, 32, 384], P(('groups', 'patch'), ('band', 'width')), parts along dimension 0
There are 2 independent parts, one for each index of `groups`. A program takes and returns all parts, laid end to end along the dimension named above; an argument that names none is the same for every part. Nothing has to cross between parts.
Inputs may be any that keep to these rules, and one draw needn't show every extreme that they name: `encode_source`: slot e < 256 holds e. `encode_target`: row and column of the extended index lie within 4 cells of the device's own block. `mesh_sender`: row and column lie in the 3 x 3 neighbourhood of blocks around the receiving block. `decode_source`: row and column of the extended index lie within one cell of the device's own block.
All inputs are finite; a program needn't handle non-finite values.
Results may differ from a plain program's by a relative error of at most 0.0095.
Values may be sent and summed in bfloat16 or wider, within the bound.
A program may use at most 64 MiB of HBM per device.

v0:
```python
import jax
import jax.numpy as jnp
from jax import lax
from jax.sharding import PartitionSpec as P

epsilon = 1e-05


def padded_2(value, sides, width):
    for axis, dim in sides:
        size, length = (lax.axis_size(axis), value.shape[dim])
        up = [(i, (i + 1) % size) for i in range(size)]
        down = [(j, i) for i, j in up]
        last = lax.slice_in_dim(value, length - width, length, axis=dim)
        initial = lax.slice_in_dim(value, 0, width, axis=dim)
        before = lax.ppermute(last, axis, up)
        after = lax.ppermute(initial, axis, down)
        value = jnp.concatenate([before, value, after], axis=dim)
    return value


def project(rows, weight):
    return jnp.dot(rows, weight, preferred_element_type=jnp.float32)


def finish(summed, bias_layer, w_out, gain_layer):
    hidden = jax.nn.silu(summed + bias_layer).astype(jnp.bfloat16)
    result = jnp.dot(hidden, w_out, preferred_element_type=jnp.float32)
    centre = jnp.mean(result, axis=-1, keepdims=True)
    shifted = result - centre
    variance = jnp.mean(shifted * shifted, axis=-1, keepdims=True)
    return shifted * lax.rsqrt(variance + epsilon) * gain_layer


def segment_total(messages, targets, valid_slot, node_count):
    node_ids = lax.broadcasted_iota(jnp.int32, (node_count, targets.shape[0]), 0)
    onehot = ((node_ids == targets[None, :]) & valid_slot[None, :]).astype(jnp.bfloat16)
    return jnp.dot(onehot, messages, preferred_element_type=jnp.float32)


def extended_projection(block, weight):
    mesh_side = block.shape[0]
    feature_width = block.shape[2]
    extended = padded_2(block, (("patch", 0), (("band", "width"), 1)), mesh_side)
    return project(extended.reshape(-1, feature_width), weight)


def return_sums(partial_value, mesh_side):
    padded = padded_2(partial_value, (("patch", 0), (("band", "width"), 1)), mesh_side)
    total = jnp.zeros((mesh_side, mesh_side, partial_value.shape[2]), jnp.float32)
    for row_block in range(3):
        for col_block in range(3):
            row_start = 2 * row_block * mesh_side
            col_start = 2 * col_block * mesh_side
            total = (
                total + padded[row_start : row_start + mesh_side, col_start : col_start + mesh_side]
            )
    return total


def per_device(
    grid_latent,
    mesh_latent,
    w_first,
    first_bias,
    w_second,
    norm_gain,
    encode_source,
    encode_target,
    encode_count,
    mesh_sender,
    mesh_receiver,
    decode_source,
):
    full_first, full_second = (
        lax.all_gather(w_first, "width", axis=2, tiled=True),
        lax.all_gather(w_second, "width", axis=2, tiled=True),
    )

    def layer_of(layer_index):
        return (first_bias[layer_index], full_second[layer_index], norm_gain[layer_index])

    feature_width = grid_latent.shape[1]
    mesh_side = mesh_latent.shape[0]
    mesh_nodes = mesh_side * mesh_side
    mesh_flat = mesh_latent.reshape(mesh_nodes, feature_width)
    grid_sending = project(grid_latent, full_first[0][:feature_width])
    mesh_receiving = extended_projection(mesh_latent, full_first[0][feature_width:])
    sources = encode_source.reshape(-1)
    targets = encode_target.reshape(-1)
    slot_ids = lax.broadcasted_iota(jnp.int32, targets.shape, 0)
    valid_slot = slot_ids < encode_count.reshape(())
    messages = finish(grid_sending[sources] + mesh_receiving[targets], *layer_of(0)).astype(
        jnp.bfloat16
    )
    partial_value = segment_total(messages, targets, valid_slot, 9 * mesh_nodes).reshape(
        3 * mesh_side, 3 * mesh_side, feature_width
    )
    encode_sum = return_sums(partial_value, mesh_side).reshape(mesh_nodes, feature_width)
    encode_low = encode_sum.astype(jnp.bfloat16)
    mesh_one = (
        mesh_flat.astype(jnp.float32)
        + finish(
            project(mesh_flat, full_first[1][:feature_width])
            + project(encode_low, full_first[1][feature_width:]),
            *layer_of(1)
        )
    ).astype(jnp.bfloat16)
    sender_terms = extended_projection(
        mesh_one.reshape(mesh_side, mesh_side, feature_width), full_first[2][:feature_width]
    )
    receiver_terms = project(mesh_one, full_first[2][feature_width:])
    receiver_ids = mesh_receiver.reshape(-1)
    edge_messages = finish(
        sender_terms[mesh_sender.reshape(-1)] + receiver_terms[receiver_ids], *layer_of(2)
    ).astype(jnp.bfloat16)
    all_valid = jnp.ones(receiver_ids.shape, jnp.bool_)
    mesh_sum = segment_total(edge_messages, receiver_ids, all_valid, mesh_nodes)
    mesh_low = mesh_sum.astype(jnp.bfloat16)
    mesh_two = (
        mesh_one.astype(jnp.float32)
        + finish(
            project(mesh_one, full_first[3][:feature_width])
            + project(mesh_low, full_first[3][feature_width:]),
            *layer_of(3)
        )
    ).astype(jnp.bfloat16)
    mesh_giving = extended_projection(
        mesh_two.reshape(mesh_side, mesh_side, feature_width), full_first[4][:feature_width]
    )
    grid_taking = project(grid_latent, full_first[4][feature_width:])
    degree = decode_source.shape[3]
    source_table = decode_source.reshape(-1, degree)
    decode_sum = jnp.zeros(grid_taking.shape, jnp.float32)
    for slot_index in range(degree):
        message = finish(
            mesh_giving[source_table[:, slot_index]] + grid_taking, *layer_of(4)
        ).astype(jnp.bfloat16)
        decode_sum = decode_sum + lax.optimization_barrier(message).astype(jnp.float32)
    grid_out = (grid_latent.astype(jnp.float32) + decode_sum).astype(jnp.bfloat16)
    return (grid_out, mesh_two.reshape(mesh_side, mesh_side, feature_width))


def solution(mesh):
    in_specs = (
        P(("groups", "patch", "band", "width"), None),
        P(("groups", "patch"), ("band", "width"), None),
        P(None, None, "width"),
        P(),
        P(None, None, "width"),
        P(),
        P("patch", ("band", "width"), None),
        P("patch", ("band", "width"), None),
        P("patch", ("band", "width")),
        P("patch", ("band", "width"), None),
        P("patch", ("band", "width"), None),
        P("patch", ("band", "width"), None, None),
    )
    out_specs = (
        P(("groups", "patch", "band", "width"), None),
        P(("groups", "patch"), ("band", "width"), None),
    )
    return jax.shard_map(
        per_device, mesh=mesh, in_specs=in_specs, out_specs=out_specs, check_vma=False
    )
```

profile of v0, /device:TPU:0, one launch (start us, length us, event | category | flops | bytes accessed | tf_op | source)
XLA Modules:
  0.0 119.2 jit_solution(9210522743436467140)
XLA Ops:
  7.9 3.1 %collective-permute-start = (bf16[8,8,384]{2,1,0:T(8,128)(2,1)}, bf16[8,8,384]{2,1,0:T(8,128)(2,1)S(1)}, u32[]{:S(2)}, u32[]{:S(2)}) collective-permute-start(bf16[8,8,384]{2,1,0:T(8,128)(2,1)} %param.13), channel_id=1, source_target_pairs={{0,4},{4,8},{8,12},{12,0},{1,5},{5,9},{9,13},{13,1},{2,6},{6,10},{... | collective-permute-start | bytes 147464 | tf_op jit(solution)/shard_map/ppermute | solution.py:16
  11.0 2.1 %collective-permute-start.1 = (bf16[8,8,384]{2,1,0:T(8,128)(2,1)}, bf16[8,8,384]{2,1,0:T(8,128)(2,1)S(1)}, u32[]{:S(2)}, u32[]{:S(2)}) collective-permute-start(bf16[8,8,384]{2,1,0:T(8,128)(2,1)} %param.13), channel_id=1, source_target_pairs={{4,0},{8,4},{12,8},{0,12},{5,1},{9,5},{13,9},{1,13},{6,2},{10,6},{... | collective-permute-start | bytes 147464 | tf_op jit(solution)/shard_map/ppermute | solution.py:17
  16.8 1.7 %collective-permute-start.3 = (bf16[24,8,384]{2,1,0:T(8,128)(2,1)S(1)}, bf16[24,8,384]{2,1,0:T(8,128)(2,1)S(1)}, u32[]{:S(2)}, u32[]{:S(2)}) collective-permute-start(bf16[24,8,384]{2,1,0:T(8,128)(2,1)S(1)} %constant_dynamic-update-slice_fusion), channel_id=1, source_target_pairs={{1,0},{2,1},{3,2},{0,3},{5,4},{6,5},{7,6},{4,7},{9,8},{10,9},{11,1... | collective-permute-start | bytes 442376 | tf_op jit(solution)/shard_map/ppermute | solution.py:17
  19.5 1.8 %collective-permute-done.2 = bf16[24,8,384]{2,1,0:T(8,128)(2,1)S(1)} collective-permute-done((bf16[24,8,384]{2,1,0:T(8,128)(2,1)S(1)}, bf16[24,8,384]{2,1,0:T(8,128)(2,1)S(1)}, u32[]{:S(2)}, u32[]{:S(2)}) %collective-permute-start.2) | collective-permute-done | bytes 147488 | tf_op jit(solution)/shard_map/ppermute | solution.py:16
  22.1 2.0 %all-gather.3.cloned.1.call-done = bf16[5,768,384]{1,2,0:T(8,128)(2,1)} async-done(((bf16[5,768,192]{1,2,0:T(8,128)(2,1)}), bf16[5,768,384]{1,2,0:T(8,128)(2,1)}) %all-gather.3.cloned.1.call-update) | async-done | bytes 2949136 | tf_op jit(solution)/shard_map/all_gather | solution.py:76
  25.5 1.6 %gather_fusion.1 = f32[512,384]{1,0:T(8,128)S(1)} fusion(f32[576,384]{1,0:T(8,128)S(1)} %fusion.25, s32[1024]{0:T(1024)S(1)} %get-tuple-element.41), kind=kCustom, calls=%fused_computation.1 | custom fusion | bytes 1574912 | tf_op jit(solution)/shard_map/gather | solution.py:93
  28.4 1.6 %gather_fusion = f32[512,384]{1,0:T(8,128)S(1)} fusion(f32[256,384]{1,0:T(8,128)S(1)} %fusion.26, s32[1024]{0:T(1024)S(1)} %pad_clamp_fusion.6), kind=kCustom, calls=%fused_computation | custom fusion | bytes 1574912 | tf_op jit(solution)/shard_map/gather | solution.py:93
  30.0 6.5 %all-gather.5.cloned.1.call-done = bf16[5,384,384]{1,2,0:T(8,128)(2,1)} async-done(((bf16[5,384,192]{1,2,0:T(8,128)(2,1)}), bf16[5,384,384]{1,2,0:T(8,128)(2,1)}) %all-gather.5.cloned.1.call-update) | async-done | bytes 1474576 | tf_op jit(solution)/shard_map/all_gather | solution.py:77
  38.8 1.8 %collective-permute-start.4 = (f32[8,24,384]{2,1,0:T(8,128)S(1)}, f32[8,24,384]{2,1,0:T(8,128)S(1)}, u32[]{:S(2)}, u32[]{:S(2)}) collective-permute-start(f32[8,24,384]{2,1,0:T(8,128)S(1)} %bitcast.128), channel_id=1, source_target_pairs={{0,4},{4,8},{8,12},{12,0},{1,5},{5,9},{9,13},{13,1},{2,6},{6,10},{... | collective-permute-start | bytes 884744 | tf_op jit(solution)/shard_map/ppermute | solution.py:16
  40.6 2.1 %collective-permute-start.5 = (f32[8,24,384]{2,1,0:T(8,128)S(1)}, f32[8,24,384]{2,1,0:T(8,128)S(1)}, u32[]{:S(2)}, u32[]{:S(2)}) collective-permute-start(f32[8,24,384]{2,1,0:T(8,128)S(1)} %bitcast.127), channel_id=1, source_target_pairs={{4,0},{8,4},{12,8},{0,12},{5,1},{9,5},{13,9},{1,13},{6,2},{10,6},{... | collective-permute-start | bytes 884744 | tf_op jit(solution)/shard_map/ppermute | solution.py:17
  42.7 7.8 %collective-permute-done.4 = f32[8,24,384]{2,1,0:T(8,128)S(1)} collective-permute-done((f32[8,24,384]{2,1,0:T(8,128)S(1)}, f32[8,24,384]{2,1,0:T(8,128)S(1)}, u32[]{:S(2)}, u32[]{:S(2)}) %collective-permute-start.4) | collective-permute-done | bytes 294944 | tf_op jit(solution)/shard_map/ppermute | solution.py:16
  50.5 5.3 %collective-permute-done.5 = f32[8,24,384]{2,1,0:T(8,128)S(1)} collective-permute-done((f32[8,24,384]{2,1,0:T(8,128)S(1)}, f32[8,24,384]{2,1,0:T(8,128)S(1)}, u32[]{:S(2)}, u32[]{:S(2)}) %collective-permute-start.5) | collective-permute-done | bytes 294944 | tf_op jit(solution)/shard_map/ppermute | solution.py:17
  56.0 1.7 %collective-permute-start.7 = (f32[40,8,384]{2,1,0:T(8,128)S(1)}, f32[40,8,384]{2,1,0:T(8,128)S(1)}, u32[]{:S(2)}, u32[]{:S(2)}) collective-permute-start(f32[40,8,384]{2,1,0:T(8,128)S(1)} %get-tuple-element.13), channel_id=1, source_target_pairs={{1,0},{2,1},{3,2},{0,3},{5,4},{6,5},{7,6},{4,7},{9,8},{10,9},{11,1... | collective-permute-start | bytes 1474568 | tf_op jit(solution)/shard_map/ppermute | solution.py:17
  58.9 8.7 %collective-permute-done.6 = f32[40,8,384]{2,1,0:T(8,128)S(1)} collective-permute-done((f32[40,8,384]{2,1,0:T(8,128)S(1)}, f32[40,8,384]{2,1,0:T(8,128)S(1)}, u32[]{:S(2)}, u32[]{:S(2)}) %collective-permute-start.6) | collective-permute-done | bytes 491552 | tf_op jit(solution)/shard_map/ppermute | solution.py:16
  68.5 1.6 %fusion.53 = (f32[64]{0:T(128)S(1)}, f32[64,384]{1,0:T(8,128)S(1)}) fusion(bf16[5,384,384]{1,2,0:T(8,128)(2,1)} %all-gather.5.cloned.1.call-done, f32[64,384]{1,0:T(8,128)S(1)} %fusion.27, bf16[5,768,384]{1,2,0:T(8,128)(2,1)} %all-gather.3.cloned.1.call-done, f32[384]{0:T(512)S(1)} %get-tuple-element.44, f32[40,8,384]{2,1,0:T(8,128)S(1)} %collective-permute-done.7, ...), kind=kOutput, calls=%fused_computation.153 | convolution fusion | flops 38166464 | bytes 1673472 | tf_op jit(solution)/shard_map/dot_general | solution.py:28
  71.6 2.7 %collective-permute-start.9 = (bf16[8,8,384]{2,1,0:T(8,128)(2,1)S(1)}, bf16[8,8,384]{2,1,0:T(8,128)(2,1)S(1)}, u32[]{:S(2)}, u32[]{:S(2)}) collective-permute-start(bf16[8,8,384]{2,1,0:T(8,128)(2,1)S(1)} %bitcast.124), channel_id=1, source_target_pairs={{4,0},{8,4},{12,8},{0,12},{5,1},{9,5},{13,9},{1,13},{6,2},{10,6},{... | collective-permute-start | bytes 147464 | tf_op jit(solution)/shard_map/ppermute | solution.py:17
  75.4 1.6 %gather_fusion.3 = f32[512,384]{1,0:T(8,128)S(1)} fusion(f32[64,384]{1,0:T(8,128)S(1)} %fusion.21, s32[1024]{0:T(1024)S(1)} %get-tuple-element.39), kind=kCustom, calls=%fused_computation.3 | custom fusion | bytes 1574912 | tf_op jit(solution)/shard_map/gather | solution.py:115
  80.1 1.6 %collective-permute-done.10 = bf16[24,8,384]{2,1,0:T(8,128)(2,1)S(1)} collective-permute-done((bf16[24,8,384]{2,1,0:T(8,128)(2,1)S(1)}, bf16[24,8,384]{2,1,0:T(8,128)(2,1)S(1)}, u32[]{:S(2)}, u32[]{:S(2)}) %collective-permute-start.10) | collective-permute-done | bytes 147488 | tf_op jit(solution)/shard_map/ppermute | solution.py:16
  83.9 1.6 %gather_fusion.2 = f32[512,384]{1,0:T(8,128)S(1)} fusion(f32[576,384]{1,0:T(8,128)S(1)} %fusion.22, s32[1024]{0:T(1024)S(1)} %get-tuple-element.40), kind=kCustom, calls=%fused_computation.2 | custom fusion | bytes 1574912 | tf_op jit(solution)/shard_map/gather | solution.py:115
  87.2 1.5 %multiply_convert_fusion.18 = bf16[64,384]{1,0:T(8,128)(2,1)S(1)} fusion(f32[64,384]{1,0:T(8,128)S(1)} %fusion.23, bf16[5,768,384]{1,2,0:T(8,128)(2,1)} %all-gather.3.cloned.1.call-done, f32[512,384]{0,1:T(8,128)S(1)} %get-tuple-element.27, f32[384]{0:T(512)S(1)} %get-tuple-element.3, f32[512]{0:T(512)S(1)} %add_rsqrt_fusion, ...), kind=kOutput, calls=%fused_computation.92 | convolution fusion | flops 45056000 | bytes 1238016 | tf_op jit(solution)/shard_map/dot_general | solution.py:23
  90.4 3.8 %collective-permute-start.13 = (bf16[8,8,384]{2,1,0:T(8,128)(2,1)S(1)}, bf16[8,8,384]{2,1,0:T(8,128)(2,1)S(1)}, u32[]{:S(2)}, u32[]{:S(2)}) collective-permute-start(bf16[8,8,384]{2,1,0:T(8,128)(2,1)S(1)} %fusion.37), channel_id=1, source_target_pairs={{4,0},{8,4},{12,8},{0,12},{5,1},{9,5},{13,9},{1,13},{6,2},{10,6},{... | collective-permute-start | bytes 147464 | tf_op jit(solution)/shard_map/ppermute | solution.py:17
  94.2 2.6 %collective-permute-done.12 = bf16[8,8,384]{2,1,0:T(8,128)(2,1)S(1)} collective-permute-done((bf16[8,8,384]{2,1,0:T(8,128)(2,1)S(1)}, bf16[8,8,384]{2,1,0:T(8,128)(2,1)S(1)}, u32[]{:S(2)}, u32[]{:S(2)}) %collective-permute-start.12) | collective-permute-done | bytes 49184 | tf_op jit(solution)/shard_map/ppermute | solution.py:16
  97.0 1.7 %collective-permute-start.15 = (bf16[24,8,384]{2,1,0:T(8,128)(2,1)S(1)}, bf16[24,8,384]{2,1,0:T(8,128)(2,1)S(1)}, u32[]{:S(2)}, u32[]{:S(2)}) collective-permute-start(bf16[24,8,384]{2,1,0:T(8,128)(2,1)S(1)} %pad_maximum_fusion.7), channel_id=1, source_target_pairs={{1,0},{2,1},{3,2},{0,3},{5,4},{6,5},{7,6},{4,7},{9,8},{10,9},{11,1... | collective-permute-start | bytes 442376 | tf_op jit(solution)/shard_map/ppermute | solution.py:17
  99.9 1.6 %collective-permute-done.14 = bf16[24,8,384]{2,1,0:T(8,128)(2,1)S(1)} collective-permute-done((bf16[24,8,384]{2,1,0:T(8,128)(2,1)S(1)}, bf16[24,8,384]{2,1,0:T(8,128)(2,1)S(1)}, u32[]{:S(2)}, u32[]{:S(2)}) %collective-permute-start.14) | collective-permute-done | bytes 147488 | tf_op jit(solution)/shard_map/ppermute | solution.py:16
  (97 shorter events, 35.9 us)
Async XLA Ops:
  7.2 16.9 %all-gather.3.cloned.1.call-start = ((), (), s32[]{:S(2)}) async-start(), calls=%async_computation | async-start | bytes 4423680 | tf_op jit(solution)/shard_map/all_gather | solution.py:76
  7.9 28.6 %all-gather.5.cloned.1.call-start = ((), (), s32[]{:S(2)}) async-start(), calls=%async_computation.1 | async-start | bytes 2211840 | tf_op jit(solution)/shard_map/all_gather | solution.py:77
  7.9 7.9 %collective-permute-start = (bf16[8,8,384]{2,1,0:T(8,128)(2,1)}, bf16[8,8,384]{2,1,0:T(8,128)(2,1)S(1)}, u32[]{:S(2)}, u32[]{:S(2)}) collective-permute-start(bf16[8,8,384]{2,1,0:T(8,128)(2,1)} %param.13), channel_id=1, source_target_pairs={{0,4},{4,8},{8,12},{12,0},{1,5},{5,9},{9,13},{13,1},{2,6},{6,10},{... | collective-permute-start | bytes 147464 | tf_op jit(solution)/shard_map/ppermute | solution.py:16
  11.0 5.7 %collective-permute-start.1 = (bf16[8,8,384]{2,1,0:T(8,128)(2,1)}, bf16[8,8,384]{2,1,0:T(8,128)(2,1)S(1)}, u32[]{:S(2)}, u32[]{:S(2)}) collective-permute-start(bf16[8,8,384]{2,1,0:T(8,128)(2,1)} %param.13), channel_id=1, source_target_pairs={{4,0},{8,4},{12,8},{0,12},{5,1},{9,5},{13,9},{1,13},{6,2},{10,6},{... | collective-permute-start | bytes 147464 | tf_op jit(solution)/shard_map/ppermute | solution.py:17
  16.7 4.6 %collective-permute-start.2 = (bf16[24,8,384]{2,1,0:T(8,128)(2,1)S(1)}, bf16[24,8,384]{2,1,0:T(8,128)(2,1)S(1)}, u32[]{:S(2)}, u32[]{:S(2)}) collective-permute-start(bf16[24,8,384]{2,1,0:T(8,128)(2,1)S(1)} %constant_dynamic-update-slice_fusion), channel_id=1, source_target_pairs={{0,1},{1,2},{2,3},{3,0},{4,5},{5,6},{6,7},{7,4},{8,9},{9,10},{10,1... | collective-permute-start | bytes 442376 | tf_op jit(solution)/shard_map/ppermute | solution.py:16
  16.8 5.3 %collective-permute-start.3 = (bf16[24,8,384]{2,1,0:T(8,128)(2,1)S(1)}, bf16[24,8,384]{2,1,0:T(8,128)(2,1)S(1)}, u32[]{:S(2)}, u32[]{:S(2)}) collective-permute-start(bf16[24,8,384]{2,1,0:T(8,128)(2,1)S(1)} %constant_dynamic-update-slice_fusion), channel_id=1, source_target_pairs={{1,0},{2,1},{3,2},{0,3},{5,4},{6,5},{7,6},{4,7},{9,8},{10,9},{11,1... | collective-permute-start | bytes 442376 | tf_op jit(solution)/shard_map/ppermute | solution.py:17
  25.5 1.6 %copy-start = (bf16[256,384]{1,0:T(8,128)(2,1)S(1)}, bf16[256,384]{1,0:T(8,128)(2,1)}, u32[]{:S(2)}) copy-start(bf16[256,384]{1,0:T(8,128)(2,1)} %param.12) | copy-start | bytes 589828
  30.0 8.2 %copy-start.4 = (s32[1,1,512]{2,1,0:T(1,128)S(1)}, s32[1,1,512]{2,1,0:T(1,128)}, u32[]{:S(2)}) copy-start(s32[1,1,512]{2,1,0:T(1,128)} %param.19) | copy-start | bytes 6148
  38.0 4.7 %copy-start.3 = (s32[1,1,256,3]{2,1,3,0:T(1,128)S(1)}, s32[1,1,256,3]{2,1,3,0:T(1,128)}, u32[]{:S(2)}) copy-start(s32[1,1,256,3]{2,1,3,0:T(1,128)} %param.23) | copy-start | bytes 9220
  38.0 19.7 %copy-start.5 = (s32[1,1,512]{2,1,0:T(1,128)S(1)}, s32[1,1,512]{2,1,0:T(1,128)}, u32[]{:S(2)}) copy-start(s32[1,1,512]{2,1,0:T(1,128)} %param.22) | copy-start | bytes 6148
  38.0 19.7 %copy-start.1 = (bf16[8,8,384]{2,1,0:T(8,128)(2,1)S(1)}, bf16[8,8,384]{2,1,0:T(8,128)(2,1)}, u32[]{:S(2)}) copy-start(bf16[8,8,384]{2,1,0:T(8,128)(2,1)} %param.13) | copy-start | bytes 147460
  38.8 11.7 %collective-permute-start.4 = (f32[8,24,384]{2,1,0:T(8,128)S(1)}, f32[8,24,384]{2,1,0:T(8,128)S(1)}, u32[]{:S(2)}, u32[]{:S(2)}) collective-permute-start(f32[8,24,384]{2,1,0:T(8,128)S(1)} %bitcast.128), channel_id=1, source_target_pairs={{0,4},{4,8},{8,12},{12,0},{1,5},{5,9},{9,13},{13,1},{2,6},{6,10},{... | collective-permute-start | bytes 884744 | tf_op jit(solution)/shard_map/ppermute | solution.py:16
  40.6 15.3 %collective-permute-start.5 = (f32[8,24,384]{2,1,0:T(8,128)S(1)}, f32[8,24,384]{2,1,0:T(8,128)S(1)}, u32[]{:S(2)}, u32[]{:S(2)}) collective-permute-start(f32[8,24,384]{2,1,0:T(8,128)S(1)} %bitcast.127), channel_id=1, source_target_pairs={{4,0},{8,4},{12,8},{0,12},{5,1},{9,5},{13,9},{1,13},{6,2},{10,6},{... | collective-permute-start | bytes 884744 | tf_op jit(solution)/shard_map/ppermute | solution.py:17
  55.9 11.7 %collective-permute-start.6 = (f32[40,8,384]{2,1,0:T(8,128)S(1)}, f32[40,8,384]{2,1,0:T(8,128)S(1)}, u32[]{:S(2)}, u32[]{:S(2)}) collective-permute-start(f32[40,8,384]{2,1,0:T(8,128)S(1)} %get-tuple-element.12), channel_id=1, source_target_pairs={{0,1},{1,2},{2,3},{3,0},{4,5},{5,6},{6,7},{7,4},{8,9},{9,10},{10,1... | collective-permute-start | bytes 1474568 | tf_op jit(solution)/shard_map/ppermute | solution.py:16
  56.0 12.5 %collective-permute-start.7 = (f32[40,8,384]{2,1,0:T(8,128)S(1)}, f32[40,8,384]{2,1,0:T(8,128)S(1)}, u32[]{:S(2)}, u32[]{:S(2)}) collective-permute-start(f32[40,8,384]{2,1,0:T(8,128)S(1)} %get-tuple-element.13), channel_id=1, source_target_pairs={{1,0},{2,1},{3,2},{0,3},{5,4},{6,5},{7,6},{4,7},{9,8},{10,9},{11,1... | collective-permute-start | bytes 1474568 | tf_op jit(solution)/shard_map/ppermute | solution.py:17
  70.4 6.7 %collective-permute-start.8 = (bf16[8,8,384]{2,1,0:T(8,128)(2,1)S(1)}, bf16[8,8,384]{2,1,0:T(8,128)(2,1)S(1)}, u32[]{:S(2)}, u32[]{:S(2)}) collective-permute-start(bf16[8,8,384]{2,1,0:T(8,128)(2,1)S(1)} %bitcast.123), channel_id=1, source_target_pairs={{0,4},{4,8},{8,12},{12,0},{1,5},{5,9},{9,13},{13,1},{2,6},{6,10},{... | collective-permute-start | bytes 147464 | tf_op jit(solution)/shard_map/ppermute | solution.py:16
  71.6 5.5 %collective-permute-start.9 = (bf16[8,8,384]{2,1,0:T(8,128)(2,1)S(1)}, bf16[8,8,384]{2,1,0:T(8,128)(2,1)S(1)}, u32[]{:S(2)}, u32[]{:S(2)}) collective-permute-start(bf16[8,8,384]{2,1,0:T(8,128)(2,1)S(1)} %bitcast.124), channel_id=1, source_target_pairs={{4,0},{8,4},{12,8},{0,12},{5,1},{9,5},{13,9},{1,13},{6,2},{10,6},{... | collective-permute-start | bytes 147464 | tf_op jit(solution)/shard_map/ppermute | solution.py:17
  77.1 4.6 %collective-permute-start.10 = (bf16[24,8,384]{2,1,0:T(8,128)(2,1)S(1)}, bf16[24,8,384]{2,1,0:T(8,128)(2,1)S(1)}, u32[]{:S(2)}, u32[]{:S(2)}) collective-permute-start(bf16[24,8,384]{2,1,0:T(8,128)(2,1)S(1)} %pad_maximum_fusion.6), channel_id=1, source_target_pairs={{0,1},{1,2},{2,3},{3,0},{4,5},{5,6},{6,7},{7,4},{8,9},{9,10},{10,1... | collective-permute-start | bytes 442376 | tf_op jit(solution)/shard_map/ppermute | solution.py:16
  77.4 5.0 %collective-permute-start.11 = (bf16[24,8,384]{2,1,0:T(8,128)(2,1)S(1)}, bf16[24,8,384]{2,1,0:T(8,128)(2,1)S(1)}, u32[]{:S(2)}, u32[]{:S(2)}) collective-permute-start(bf16[24,8,384]{2,1,0:T(8,128)(2,1)S(1)} %pad_maximum_fusion.6), channel_id=1, source_target_pairs={{1,0},{2,1},{3,2},{0,3},{5,4},{6,5},{7,6},{4,7},{9,8},{10,9},{11,1... | collective-permute-start | bytes 442376 | tf_op jit(solution)/shard_map/ppermute | solution.py:17
  90.3 14.2 %copy-start.2 = (bf16[8,8,384]{2,1,0:T(8,128)(2,1)}, bf16[8,8,384]{2,1,0:T(8,128)(2,1)S(1)}, u32[]{:S(2)}) copy-start(bf16[8,8,384]{2,1,0:T(8,128)(2,1)S(1)} %fusion.37) | copy-start | bytes 147460
  90.3 6.5 %collective-permute-start.12 = (bf16[8,8,384]{2,1,0:T(8,128)(2,1)S(1)}, bf16[8,8,384]{2,1,0:T(8,128)(2,1)S(1)}, u32[]{:S(2)}, u32[]{:S(2)}) collective-permute-start(bf16[8,8,384]{2,1,0:T(8,128)(2,1)S(1)} %fusion.37), channel_id=1, source_target_pairs={{0,4},{4,8},{8,12},{12,0},{1,5},{5,9},{9,13},{13,1},{2,6},{6,10},{... | collective-permute-start | bytes 147464 | tf_op jit(solution)/shard_map/ppermute | solution.py:16
  90.4 6.5 %collective-permute-start.13 = (bf16[8,8,384]{2,1,0:T(8,128)(2,1)S(1)}, bf16[8,8,384]{2,1,0:T(8,128)(2,1)S(1)}, u32[]{:S(2)}, u32[]{:S(2)}) collective-permute-start(bf16[8,8,384]{2,1,0:T(8,128)(2,1)S(1)} %fusion.37), channel_id=1, source_target_pairs={{4,0},{8,4},{12,8},{0,12},{5,1},{9,5},{13,9},{1,13},{6,2},{10,6},{... | collective-permute-start | bytes 147464 | tf_op jit(solution)/shard_map/ppermute | solution.py:17
  96.9 4.6 %collective-permute-start.14 = (bf16[24,8,384]{2,1,0:T(8,128)(2,1)S(1)}, bf16[24,8,384]{2,1,0:T(8,128)(2,1)S(1)}, u32[]{:S(2)}, u32[]{:S(2)}) collective-permute-start(bf16[24,8,384]{2,1,0:T(8,128)(2,1)S(1)} %pad_maximum_fusion.7), channel_id=1, source_target_pairs={{0,1},{1,2},{2,3},{3,0},{4,5},{5,6},{6,7},{7,4},{8,9},{9,10},{10,1... | collective-permute-start | bytes 442376 | tf_op jit(solution)/shard_map/ppermute | solution.py:16
  97.0 5.1 %collective-permute-start.15 = (bf16[24,8,384]{2,1,0:T(8,128)(2,1)S(1)}, bf16[24,8,384]{2,1,0:T(8,128)(2,1)S(1)}, u32[]{:S(2)}, u32[]{:S(2)}) collective-permute-start(bf16[24,8,384]{2,1,0:T(8,128)(2,1)S(1)} %pad_maximum_fusion.7), channel_id=1, source_target_pairs={{1,0},{2,1},{3,2},{0,3},{5,4},{6,5},{7,6},{4,7},{9,8},{10,9},{11,1... | collective-permute-start | bytes 442376 | tf_op jit(solution)/shard_map/ppermute | solution.py:17
Sparse Core Ops, SparseCore 0:
  9.5 14.5 all-gather.2
  25.6 10.8 all-gather.4
where the time goes:
time: 121 us; the launch traced here: 119 us
  waiting for transfers between devices  41.6 us (34%)
  starting transfers between devices  24 us (20%)
  matrix products  22.2 us (18%)
  between operations  15.1 us (12%)
  local copies, waits for them, and re-layouts  11.2 us (9%)
  other arithmetic  4.91 us (4%)
    ppermute x8, waiting for transfers between devices, padded_2(): before = lax.ppermute(last, axis, up)  24.2 us
    ppermute x8, starting transfers between devices, padded_2(): after = lax.ppermute(initial, axis, down)  17.3 us
    dot_general x9, matrix products, project(): return jnp.dot(rows, weight, preferred_element_type=jnp.float32)  11.8 us
    dot_general x7, matrix products, finish(): result = jnp.dot(hidden, w_out, preferred_element_type=jnp.float32)  9.9 us
    ppermute x8, waiting for transfers between devices, padded_2(): after = lax.ppermute(initial, axis, down)  8.22 us
    ppermute x8, starting transfers between devices, padded_2(): before = lax.ppermute(last, axis, up)  6.7 us
    all_gather x1, waiting for transfers between devices, per_device(): lax.all_gather(w_second, 'width', axis=2, tiled=True)  6.5 us
    gather x3, local copies, waits for them, and re-layouts, per_device(): mesh_giving[source_table[:, slot_index]] + grid_taking  2.97 us
  transfers between devices with their start and end apart: 18, of which 13 were waited for; matrix products, arithmetic and copies ran while one was open for 14% of the time, Pallas kernels for 0%

commit v1 on v0

v1 whole, which is shorter than its diff:
```python
import functools

import jax
import jax.numpy as jnp
import numpy as np
from jax import lax
from jax.experimental import pallas as pl
from jax.experimental.pallas import tpu as pltpu
from jax.sharding import PartitionSpec as P

EPSILON = 1e-05
MESH = pl.DeviceIdType.MESH
BF16 = jnp.bfloat16
F32 = jnp.float32
ENC_REACH = 4
DEC_REACH = 1
DIRS = ((1, 0), (-1, 0), (0, 1), (0, -1), (1, 1), (1, -1), (-1, 1), (-1, -1))


def span(step, side, reach):
    if step == 0:
        return list(range(side))
    return list(range(side - reach, side)) if step > 0 else list(range(reach))


def packing(side, reach):
    nodes, starts, sizes = [], [], []
    for dp, dc in DIRS:
        part = [i * side + j for i in span(dp, side, reach) for j in span(dc, side, reach)]
        part = part + [-1] * (-len(part) % 16)
        starts.append(len(nodes))
        sizes.append(len(part))
        nodes.extend(part)
    matrix = np.zeros((len(nodes), side * side), np.float32)
    for place, node in enumerate(nodes):
        if node >= 0:
            matrix[place, node] = 1.0
    return matrix, starts, sizes


def region_index(ext_ids, side, reach, starts):
    ext_side = 3 * side
    own = side * side
    row = (ext_ids * ((1 << 20) // ext_side + 1)) >> 20
    col = ext_ids - ext_side * row
    up, down = row < side, row >= 2 * side
    left, right = col < side, col >= 2 * side
    row_in = row - jnp.where(up, side - reach, jnp.where(down, 2 * side, side))
    col_in = col - jnp.where(left, side - reach, jnp.where(right, 2 * side, side))
    stride = jnp.where(left | right, reach, side)

    def base(dp):
        mid = own + starts[DIRS.index((dp, 0))] if dp else 0
        return jnp.where(
            left,
            own + starts[DIRS.index((dp, 1))],
            jnp.where(right, own + starts[DIRS.index((dp, -1))], mid),
        )

    offset = jnp.where(up, base(1), jnp.where(down, base(-1), base(0)))
    return offset + row_in * stride + col_in


def dot(a, b):
    return jnp.dot(a, b, preferred_element_type=F32)


def ones_where(mask):
    return jnp.where(mask, 1.0, 0.0).astype(BF16)


def columns_of(index_row):
    return jnp.transpose(jnp.broadcast_to(index_row, (128, index_row.shape[1])))


def onehot_columns(index_cols, width):
    pieces = []
    for begin in range(0, width, 128):
        size = min(128, width - begin)
        ids = lax.broadcasted_iota(jnp.int32, (index_cols.shape[0], size), 1) + begin
        pieces.append(ones_where(index_cols[:, :size] == ids))
    return pieces[0] if len(pieces) == 1 else jnp.concatenate(pieces, axis=1)


def kernel(
    sizes,
    grid_ref,
    block_ref,
    w_first_ref,
    bias_ref,
    w_second_ref,
    gain_ref,
    enc_source_ref,
    enc_target_ref,
    enc_count_ref,
    sender_ref,
    receiver_ref,
    dec_source_ref,
    enc_pack_ref,
    enc_unpack_ref,
    dec_pack_ref,
    grid_out_ref,
    mesh_out_ref,
    half_first,
    half_second,
    full_first,
    full_second,
    enc_send,
    enc_table,
    sum_send,
    sum_recv,
    mid_table,
    dec_send,
    dec_table,
    local_sem,
    weight_send_sem,
    weight_recv_sem,
    halo_send_sem,
    halo_recv_sem,
):
    n_patch, n_band, n_width = sizes
    n_cols = n_band * n_width
    group, patch = lax.axis_index("groups"), lax.axis_index("patch")
    band, core = lax.axis_index("band"), lax.axis_index("width")
    column = band * n_width + core
    n_layers, _, feat = full_first.shape
    own = block_ref.shape[0]
    side = int(round(own**0.5))
    _, enc_starts, enc_sizes = packing(side, ENC_REACH)
    _, dec_starts, dec_sizes = packing(side, DEC_REACH)
    mid_starts = [own * i for i in range(8)]

    def neighbour(dp, dc):
        there = lax.rem(column + dc + n_cols, n_cols)
        return (
            group,
            lax.rem(patch + dp + n_patch, n_patch),
            there // n_width,
            lax.rem(there, n_width),
        )

    partner = (group, patch, band, 1 - core)

    barrier = pltpu.get_barrier_semaphore()
    for dp, dc in DIRS:
        pl.semaphore_signal(barrier, inc=1, device_id=neighbour(dp, dc), device_id_type=MESH)

    local = []
    for k in range(n_layers):
        pair = []
        for s, (src, dst) in enumerate(((w_first_ref, half_first), (w_second_ref, half_second))):
            copy = pltpu.make_async_copy(src.at[k], dst.at[core, k], local_sem.at[s, k])
            copy.start()
            pair.append(copy)
        local.append(pair)

    block = block_ref[...]
    enc_send[...] = dot(enc_pack_ref[...], block).astype(BF16)
    enc_table[:own] = block
    pl.semaphore_wait(barrier, len(DIRS))

    def exchange(phase, source_of, target_of, towards=1):
        copies = []
        for d, (dp, dc) in enumerate(DIRS):
            copy = pltpu.make_async_remote_copy(
                src_ref=source_of(d),
                dst_ref=target_of(d),
                send_sem=halo_send_sem.at[phase, d],
                recv_sem=halo_recv_sem.at[phase, d],
                device_id=neighbour(towards * dp, towards * dc),
                device_id_type=MESH,
            )
            copy.start()
            copies.append(copy)
        return copies

    halo_copies = exchange(
        0,
        lambda d: enc_send.at[pl.ds(enc_starts[d], enc_sizes[d])],
        lambda d: enc_table.at[pl.ds(own + enc_starts[d], enc_sizes[d])],
    )
    remote = []
    for k in range(n_layers):
        pair = []
        for s, (src, dst) in enumerate(((w_first_ref, half_first), (w_second_ref, half_second))):
            copy = pltpu.make_async_remote_copy(
                src_ref=src.at[k],
                dst_ref=dst.at[core, k],
                send_sem=weight_send_sem.at[s, k],
                recv_sem=weight_recv_sem.at[s, k],
                device_id=partner,
                device_id_type=MESH,
            )
            copy.start()
            pair.append(copy)
        remote.append(pair)

    def take_weights(k):
        for s, (half, full) in enumerate(((half_first, full_first), (half_second, full_second))):
            local[k][s].wait()
            remote[k][s].wait_recv()
            full[k] = jnp.concatenate([half[0, k], half[1, k]], axis=-1)

    def upper(k):
        return full_first[k, :feat]

    def lower(k):
        return full_first[k, feat:]

    def finish(k, summed):
        half = 0.5 * summed
        hidden = (half + half * jnp.tanh(half)).astype(BF16)
        result = dot(hidden, full_second[k])
        centre = jnp.mean(result, axis=-1, keepdims=True)
        shifted = result - centre
        variance = jnp.mean(shifted * shifted, axis=-1, keepdims=True)
        return shifted * lax.rsqrt(variance + EPSILON) * gain_ref[k : k + 1, :]

    def bias(k):
        return bias_ref[k : k + 1, :]

    grid = grid_ref[...]
    n_grid = grid.shape[0]
    n_enc = enc_target_ref.shape[1]
    own_enc = min(n_grid, n_enc)
    source_cols = columns_of(enc_source_ref[...][:, own_enc:])
    more = dot(onehot_columns(source_cols, n_grid), grid).astype(BF16)
    sending = jnp.concatenate([grid, more], axis=0)
    n_enc_rows = own + sum(enc_sizes)
    target_row = region_index(enc_target_ref[...], side, ENC_REACH, enc_starts)
    target_onehot = onehot_columns(columns_of(target_row), n_enc_rows)
    slot_ids = lax.broadcasted_iota(jnp.int32, (1, n_enc), 1)
    kept_row = jnp.where(slot_ids < enc_count_ref[...], target_row, -1)
    node_ids = lax.broadcasted_iota(jnp.int32, (n_enc_rows, n_enc), 0)
    scatter = ones_where(node_ids == kept_row)
    take_weights(0)
    grid_term = dot(sending, upper(0)) + bias(0)
    for copy in halo_copies:
        copy.wait_recv()
    target_rows = dot(target_onehot, enc_table[...]).astype(BF16)
    messages = finish(0, grid_term + dot(target_rows, lower(0))).astype(BF16)
    partial = dot(scatter, messages)
    sum_send[...] = partial[own:].astype(BF16)
    sum_copies = exchange(
        1,
        lambda d: sum_send.at[pl.ds(enc_starts[d], enc_sizes[d])],
        lambda d: sum_recv.at[pl.ds(enc_starts[d], enc_sizes[d])],
        -1,
    )

    take_weights(1)
    node_term = dot(block, upper(1)) + bias(1)
    take_weights(2)
    take_weights(3)
    for copy in sum_copies:
        copy.wait_recv()
    encode_sum = partial[:own] + dot(enc_unpack_ref[...], sum_recv[...])
    node_pre = node_term + dot(encode_sum.astype(BF16), lower(1))
    mesh_one = (block.astype(F32) + finish(1, node_pre)).astype(BF16)
    mid_table[0] = mesh_one
    mid_copies = exchange(2, lambda d: mid_table.at[0], lambda d: mid_table.at[1 + d])

    receiver_row = receiver_ref[...]
    n_edges = receiver_row.shape[1]
    taking_rows = dot(onehot_columns(columns_of(receiver_row), own), mesh_one).astype(BF16)
    edge_term = dot(taking_rows, lower(2)) + bias(2)
    own_ids = lax.broadcasted_iota(jnp.int32, (own, n_edges), 0)
    edge_scatter = ones_where(own_ids == receiver_row)
    sender_row = region_index(sender_ref[...], side, side, mid_starts)
    sender_onehot = onehot_columns(columns_of(sender_row), 9 * own)
    node_term_two = dot(mesh_one, upper(3)) + bias(3)
    take_weights(4)
    grid_taking = dot(grid, lower(4)) + bias(4)
    n_dec_rows = own + sum(dec_sizes)
    for copy in mid_copies:
        copy.wait_recv()
    sending_rows = dot(sender_onehot, mid_table[...].reshape(9 * own, feat)).astype(BF16)
    edge_messages = finish(2, edge_term + dot(sending_rows, upper(2))).astype(BF16)
    mesh_sum = dot(edge_scatter, edge_messages)
    node_pre_two = node_term_two + dot(mesh_sum.astype(BF16), lower(3))
    mesh_two = (mesh_one.astype(F32) + finish(3, node_pre_two)).astype(BF16)
    mesh_out_ref[...] = mesh_two
    dec_send[...] = dot(dec_pack_ref[...], mesh_two).astype(BF16)
    dec_table[:own] = mesh_two
    dec_copies = exchange(
        3,
        lambda d: dec_send.at[pl.ds(dec_starts[d], dec_sizes[d])],
        lambda d: dec_table.at[pl.ds(own + dec_starts[d], dec_sizes[d])],
    )

    dec_rows = region_index(dec_source_ref[...], side, DEC_REACH, dec_starts)
    dec_ids = lax.broadcasted_iota(jnp.int32, (n_grid, n_dec_rows), 1)
    dec_onehots = [
        ones_where(dec_rows[:, k : k + 1] == dec_ids) for k in range(dec_rows.shape[1])
    ]
    for copy in dec_copies:
        copy.wait_recv()
    table = dec_table[...]
    total = grid.astype(F32)
    decode_sum = None
    for onehot in dec_onehots:
        giving_rows = dot(onehot, table).astype(BF16)
        message = finish(4, grid_taking + dot(giving_rows, upper(4))).astype(BF16).astype(F32)
        decode_sum = message if decode_sum is None else decode_sum + message
    grid_out_ref[...] = (total + decode_sum).astype(BF16)

    for copies in remote + [halo_copies, sum_copies, mid_copies, dec_copies]:
        for copy in copies:
            copy.wait_send()


def per_device(
    sizes,
    grid_latent,
    mesh_latent,
    w_first,
    first_bias,
    w_second,
    norm_gain,
    encode_source,
    encode_target,
    encode_count,
    mesh_sender,
    mesh_receiver,
    decode_source,
):
    side, _, feat = mesh_latent.shape
    own = side * side
    n_layers = w_first.shape[0]
    share = w_first.shape[2]
    enc_matrix, _, enc_sizes = packing(side, ENC_REACH)
    dec_matrix, _, dec_sizes = packing(side, DEC_REACH)
    n_enc, n_dec = sum(enc_sizes), sum(dec_sizes)
    vmem = pl.BlockSpec(memory_space=pltpu.VMEM)
    anywhere = pl.BlockSpec(memory_space=pl.ANY)
    grid_out, mesh_out = pl.pallas_call(
        functools.partial(kernel, sizes),
        out_shape=(
            jax.ShapeDtypeStruct(grid_latent.shape, BF16),
            jax.ShapeDtypeStruct((own, feat), BF16),
        ),
        in_specs=[vmem, vmem, anywhere, vmem, anywhere] + [vmem] * 10,
        out_specs=(vmem, vmem),
        scratch_shapes=[
            pltpu.VMEM((2, n_layers, 2 * feat, share), BF16),
            pltpu.VMEM((2, n_layers, feat, share), BF16),
            pltpu.VMEM((n_layers, 2 * feat, feat), BF16),
            pltpu.VMEM((n_layers, feat, feat), BF16),
            pltpu.VMEM((n_enc, feat), BF16),
            pltpu.VMEM((own + n_enc, feat), BF16),
            pltpu.VMEM((n_enc, feat), BF16),
            pltpu.VMEM((n_enc, feat), BF16),
            pltpu.VMEM((9, own, feat), BF16),
            pltpu.VMEM((n_dec, feat), BF16),
            pltpu.VMEM((own + n_dec, feat), BF16),
            pltpu.SemaphoreType.DMA((2, n_layers)),
            pltpu.SemaphoreType.DMA((2, n_layers)),
            pltpu.SemaphoreType.DMA((2, n_layers)),
            pltpu.SemaphoreType.DMA((4, 8)),
            pltpu.SemaphoreType.DMA((4, 8)),
        ],
        compiler_params=pltpu.CompilerParams(
            collective_id=0, has_side_effects=True, vmem_limit_bytes=48 * 1024 * 1024
        ),
    )(
        grid_latent,
        mesh_latent.reshape(own, feat),
        w_first,
        first_bias,
        w_second,
        norm_gain,
        encode_source.reshape(1, -1),
        encode_target.reshape(1, -1),
        encode_count.reshape(1, 1),
        mesh_sender.reshape(1, -1),
        mesh_receiver.reshape(1, -1),
        decode_source.reshape(decode_source.shape[2:]),
        jnp.asarray(enc_matrix, BF16),
        jnp.asarray(enc_matrix.T, BF16),
        jnp.asarray(dec_matrix, BF16),
    )
    return grid_out, mesh_out.reshape(mesh_latent.shape)


def solution(mesh):
    sizes = tuple(mesh.shape[name] for name in ("patch", "band", "width"))
    in_specs = (
        P(("groups", "patch", "band", "width"), None),
        P(("groups", "patch"), ("band", "width"), None),
        P(None, None, "width"),
        P(),
        P(None, None, "width"),
        P(),
        P("patch", ("band", "width"), None),
        P("patch", ("band", "width"), None),
        P("patch", ("band", "width")),
        P("patch", ("band", "width"), None),
        P("patch", ("band", "width"), None),
        P("patch", ("band", "width"), None, None),
    )
    out_specs = (
        P(("groups", "patch", "band", "width"), None),
        P(("groups", "patch"), ("band", "width"), None),
    )
    return jax.shard_map(
        functools.partial(per_device, sizes),
        mesh=mesh,
        in_specs=in_specs,
        out_specs=out_specs,
        check_vma=False,
    )
```

time: 121 us -> 45 us (0.37); the launches traced: 119 us -> 44.8 us
  waiting for transfers between devices: 41.6 us -> 0 us
  Pallas kernels: 0 us -> 36.6 us
  starting transfers between devices: 24 us -> 0 us
  matrix products: 22.2 us -> 0 us
  between operations: 15.1 us -> 1.48 us
  other arithmetic: 4.91 us -> 0 us
  local copies, waits for them, and re-layouts: 11.2 us -> 6.69 us
    pallas_call x0 -> x1, Pallas kernels: none -> 36.6 us  [per_device(): pl.pallas_call(functools.partial(kernel, sizes), out_shape=(jax.ShapeDtyp...]
    ppermute x16 -> x0, waiting for transfers between devices: 32.5 us -> none  [the longest x8 24.2 us: padded_2(): before = lax.ppermute(last, axis, up)]
    ppermute x16 -> x0, starting transfers between devices: 24 us -> none  [the longest x8 17.3 us: padded_2(): after = lax.ppermute(initial, axis, down)]
    dot_general x17 -> x0, matrix products: 22.2 us -> none  [the longest x9 11.8 us: project(): return jnp.dot(rows, weight, preferred_element_type=jnp.float32)]
    gather x7 -> x0, local copies, waits for them, and re-layouts: 9.35 us -> none  [the longest x3 2.97 us: per_device(): mesh_giving[source_table[:, slot_index]] + grid_taking]
    all_gather x2 -> x0, waiting for transfers between devices: 8.48 us -> none  [the longest x1 6.5 us: per_device(): lax.all_gather(w_second, 'width', axis=2, tiled=True)]
    unnamed x15 -> x27, local copies, waits for them, and re-layouts: 0.86 us -> 6.69 us
    select_n x5 -> x0, other arithmetic: 2.07 us -> none  [the longest x1 0.69 us: per_device(): mesh_receiving[targets]]
  transfers between devices with their start and end apart: 18 -> 0, of which waited for: 13 -> 0; matrix products, arithmetic and copies ran while one was open for 14% -> 0% of each run, Pallas kernels for 0% -> 0%
where the time goes in v1:
time: 45 us; the launch traced here: 44.8 us
  Pallas kernels  36.6 us (81%)
  local copies, waits for them, and re-layouts  6.69 us (15%)
  between operations  1.48 us (3%)
    pallas_call x1, Pallas kernels, per_device(): pl.pallas_call(functools.partial(kernel, sizes), out_shape=(jax.ShapeDtyp...  36.6 us
    unnamed x27, local copies, waits for them, and re-layouts  6.69 us

profile of v1, /device:TPU:0, one launch (start us, length us, event | category | flops | bytes accessed | tf_op | source)
XLA Modules:
  0.0 44.8 jit_solution(3707926427215286978)
XLA Ops:
  1.3 0.8 %copy.17 = s32[1,1,256,3]{3,2,1,0:T(8,128)S(1)} copy(s32[1,1,256,3]{2,1,3,0:T(1,128)} %param.26) | data formatting | bytes 6144 | tf_op args[11]
  2.1 1.8 %copy.19.w_second_ref = bf16[5,384,192]{2,1,0:T(8,128)(2,1)S(1)} copy(bf16[5,384,192]{1,2,0:T(8,128)(2,1)} %param.19) | data formatting | bytes 1474560 | tf_op args[4]
  3.9 0.0 copy-start
  4.0 0.0 copy-start.1
  4.0 0.0 copy-start.2
  4.0 0.0 copy-start.3
  4.0 0.0 copy-start.4
  4.0 0.0 copy-start.5
  4.0 0.0 copy-start.6
  4.0 0.0 copy-start.7
  4.0 0.0 copy-start.8
  4.1 0.0 copy-start.9
  4.1 0.0 copy-start.10
  4.1 2.7 %copy.18.w_first_ref = bf16[5,768,192]{2,1,0:T(8,128)(2,1)S(1)} copy(bf16[5,768,192]{1,2,0:T(8,128)(2,1)} %param.17) | data formatting | bytes 2949120 | tf_op args[2]
  6.8 0.0 copy-done
  6.8 0.0 copy-done.1
  6.8 0.0 copy-done.2
  6.8 0.0 copy-done.3
  6.8 0.0 copy-done.4
  6.8 0.0 copy-done.5
  6.8 0.0 copy-done.6
  6.9 36.6 %shard_map.158 = (bf16[256,384]{1,0:T(8,128)(2,1)S(1)}, bf16[64,384]{1,0:T(8,128)(2,1)S(1)}) custom-call(bf16[256,384]{1,0:T(8,128)(2,1)S(1)} %copy-done, bf16[64,384]{1,0:T(8,128)(2,1)S(1)} %bitcast.9, bf16[5,768,192]{2,1,0:T(8,128)(2,1)S(1)} %copy.18.w_first_ref, f32[5,384]{1,0:T(8,128)S(1)} %copy-done.5, bf16[5,384,192]{2,1,0:T(8,128)(2,1)S(1)} %copy.19.w_second_ref, ...), custom_call_target="tpu_custom_call" | custom-call | tf_op jit(solution)/shard_map/pallas_call | solution.py:336
  43.5 0.7 %copy.23 = bf16[256,384]{1,0:T(8,128)(2,1)} copy(bf16[256,384]{1,0:T(8,128)(2,1)S(1)} %get-tuple-element.8) | data formatting | bytes 393216
  44.2 0.6 %copy.24 = bf16[8,8,384]{2,1,0:T(8,128)(2,1)} copy(bf16[8,8,384]{2,1,0:T(8,128)(2,1)S(1)} %bitcast.8) | data formatting | bytes 98304
  (4 shorter events, 0.0 us)
Async XLA Ops:
  3.9 2.8 %copy-start = (bf16[256,384]{1,0:T(8,128)(2,1)S(1)}, bf16[256,384]{1,0:T(8,128)(2,1)}, u32[]{:S(2)}) copy-start(bf16[256,384]{1,0:T(8,128)(2,1)} %grid_ref.1) | copy-start | bytes 589828
  4.0 2.8 %copy-start.1 = (bf16[8,8,384]{2,1,0:T(8,128)(2,1)S(1)}, bf16[8,8,384]{2,1,0:T(8,128)(2,1)}, u32[]{:S(2)}) copy-start(bf16[8,8,384]{2,1,0:T(8,128)(2,1)} %param.16) | copy-start | bytes 147460
  4.0 2.8 %copy-start.2 = (bf16[192,64]{1,0:T(8,128)(2,1)S(1)}, bf16[192,64]{1,0:T(8,128)(2,1)}, u32[]{:S(2)}) copy-start(bf16[192,64]{1,0:T(8,128)(2,1)} %constant.6.clone.enc_pack_ref) | copy-start | bytes 73732
  4.0 2.8 %copy-start.3 = (bf16[128,64]{1,0:T(8,128)(2,1)S(1)}, bf16[128,64]{1,0:T(8,128)(2,1)}, u32[]{:S(2)}) copy-start(bf16[128,64]{1,0:T(8,128)(2,1)} %constant.8.clone.dec_pack_ref) | copy-start | bytes 49156
  4.0 2.8 %copy-start.4 = (bf16[64,192]{1,0:T(8,128)(2,1)S(1)}, bf16[64,192]{1,0:T(8,128)(2,1)}, u32[]{:S(2)}) copy-start(bf16[64,192]{1,0:T(8,128)(2,1)} %constant.7.clone.enc_unpack_ref) | copy-start | bytes 73732
  4.0 2.8 %copy-start.5 = (f32[5,384]{1,0:T(8,128)S(1)}, f32[5,384]{1,0:T(8,128)}, u32[]{:S(2)}) copy-start(f32[5,384]{1,0:T(8,128)} %bias_ref.1) | copy-start | bytes 23044
  4.0 2.8 %copy-start.6 = (f32[5,384]{1,0:T(8,128)S(1)}, f32[5,384]{1,0:T(8,128)}, u32[]{:S(2)}) copy-start(f32[5,384]{1,0:T(8,128)} %gain_ref.1) | copy-start | bytes 23044
  4.0 2.8 %copy-start.7 = (s32[1,1,512]{2,1,0:T(1,128)S(1)}, s32[1,1,512]{2,1,0:T(1,128)}, u32[]{:S(2)}) copy-start(s32[1,1,512]{2,1,0:T(1,128)} %param.21) | copy-start | bytes 6148
  4.0 2.8 %copy-start.8 = (s32[1,1,512]{2,1,0:T(1,128)S(1)}, s32[1,1,512]{2,1,0:T(1,128)}, u32[]{:S(2)}) copy-start(s32[1,1,512]{2,1,0:T(1,128)} %param.22) | copy-start | bytes 6148
  4.1 2.8 %copy-start.9 = (s32[1,1,512]{2,1,0:T(1,128)S(1)}, s32[1,1,512]{2,1,0:T(1,128)}, u32[]{:S(2)}) copy-start(s32[1,1,512]{2,1,0:T(1,128)} %param.24) | copy-start | bytes 6148
  4.1 2.8 %copy-start.10 = (s32[1,1,512]{2,1,0:T(1,128)S(1)}, s32[1,1,512]{2,1,0:T(1,128)}, u32[]{:S(2)}) copy-start(s32[1,1,512]{2,1,0:T(1,128)} %param.25) | copy-start | bytes 6148

commit v2 on v1

--- a/solution.py
+++ b/solution.py
@@ -65,6 +65,10 @@
     return jnp.dot(a, b, preferred_element_type=F32)
 
 
+def dot_t(a, b):
+    return lax.dot_general(a, b, (((1,), (1,)), ((), ())), preferred_element_type=F32)
+
+
 def ones_where(mask):
     return jnp.where(mask, 1.0, 0.0).astype(BF16)
 
@@ -82,48 +86,54 @@
     return pieces[0] if len(pieces) == 1 else jnp.concatenate(pieces, axis=1)
 
 
-def kernel(
-    sizes,
-    grid_ref,
-    block_ref,
-    w_first_ref,
-    bias_ref,
-    w_second_ref,
-    gain_ref,
-    enc_source_ref,
-    enc_target_ref,
-    enc_count_ref,
-    sender_ref,
-    receiver_ref,
-    dec_source_ref,
-    enc_pack_ref,
-    enc_unpack_ref,
-    dec_pack_ref,
-    grid_out_ref,
-    mesh_out_ref,
-    half_first,
-    half_second,
-    full_first,
-    full_second,
-    enc_send,
-    enc_table,
-    sum_send,
-    sum_recv,
-    mid_table,
-    dec_send,
-    dec_table,
-    local_sem,
-    weight_send_sem,
-    weight_recv_sem,
-    halo_send_sem,
-    halo_recv_sem,
-):
+STAGED = 13
+
+
+def kernel(sizes, *refs):
+    w_first_ref, w_second_ref = refs[:2]
+    staged_hbm = refs[2 : 2 + STAGED]
+    grid_out_ref, mesh_out_ref = refs[2 + STAGED : 4 + STAGED]
+    staged = refs[4 + STAGED : 4 + 2 * STAGED]
+    (
+        grid_ref,
+        block_ref,
+        bias_ref,
+        gain_ref,
+        enc_source_ref,
+        enc_target_ref,
+        enc_count_ref,
+        sender_ref,
+        receiver_ref,
+        dec_source_ref,
+        enc_pack_ref,
+        enc_unpack_ref,
+        dec_pack_ref,
+    ) = staged
+    (
+        full_first,
+        full_second,
+        enc_send,
+        enc_table,
+        sum_send,
+        sum_recv,
+        mid_table,
+        dec_send,
+        dec_table,
+        staged_sem,
+        local_sem,
+        weight_send_sem,
+        weight_recv_sem,
+        halo_send_sem,
+        halo_recv_sem,
+    ) = refs[4 + 2 * STAGED :]
     n_patch, n_band, n_width = sizes
     n_cols = n_band * n_width
     group, patch = lax.axis_index("groups"), lax.axis_index("patch")
     band, core = lax.axis_index("band"), lax.axis_index("width")
     column = band * n_width + core
-    n_layers, _, feat = full_first.shape
+    n_layers, feat, _ = full_first.shape
+    share = w_first_ref.shape[1]
+    own_rows = pl.ds(pl.multiple_of(core * share, 16), share)
     own = block_ref.shape[0]
     side = int(round(own**0.5))
     _, enc_starts, enc_sizes = packing(side, ENC_REACH)
@@ -145,23 +155,33 @@
     for dp, dc in DIRS:
         pl.semaphore_signal(barrier, inc=1, device_id=neighbour(dp, dc), device_id_type=MESH)
 
+    staging = []
+    for i in range(STAGED):
+        copy = pltpu.make_async_copy(staged_hbm[i], staged[i], staged_sem.at[i])
+        copy.start()
+        staging.append(copy)
     local = []
     for k in range(n_layers):
         pair = []
-        for s, (src, dst) in enumerate(((w_first_ref, half_first), (w_second_ref, half_second))):
-            copy = pltpu.make_async_copy(src.at[k], dst.at[core, k], local_sem.at[s, k])
+        for s, (src, dst) in enumerate(((w_first_ref, full_first), (w_second_ref, full_second))):
+            copy = pltpu.make_async_copy(src.at[k], dst.at[k, own_rows], local_sem.at[s, k])
             copy.start()
             pair.append(copy)
         local.append(pair)
 
+    for copy in staging:
+        copy.wait()
     block = block_ref[...]
     enc_send[...] = dot(enc_pack_ref[...], block).astype(BF16)
     enc_table[:own] = block
     pl.semaphore_wait(barrier, len(DIRS))
 
-    def exchange(phase, source_of, target_of, towards=1):
+    def exchange(phase, source_of, target_of, towards=1, chosen=None):
         copies = []
-        for d, (dp, dc) in enumerate(DIRS):
+        for d in range(len(DIRS)) if chosen is None else chosen:
+            dp, dc = DIRS[d][0], DIRS[d][1]
+            if chosen and len(chosen) < 4:
+                dp = 0
             copy = pltpu.make_async_remote_copy(
                 src_ref=source_of(d),
                 dst_ref=target_of(d),
@@ -182,10 +202,10 @@
     remote = []
     for k in range(n_layers):
         pair = []
-        for s, (src, dst) in enumerate(((w_first_ref, half_first), (w_second_ref, half_second))):
+        for s, (src, dst) in enumerate(((w_first_ref, full_first), (w_second_ref, full_second))):
             copy = pltpu.make_async_remote_copy(
                 src_ref=src.at[k],
-                dst_ref=dst.at[core, k],
+                dst_ref=dst.at[k, own_rows],
                 send_sem=weight_send_sem.at[s, k],
                 recv_sem=weight_recv_sem.at[s, k],
                 device_id=partner,
@@ -196,21 +216,20 @@
         remote.append(pair)
 
     def take_weights(k):
-        for s, (half, full) in enumerate(((half_first, full_first), (half_second, full_second))):
+        for s in range(2):
             local[k][s].wait()
             remote[k][s].wait_recv()
-            full[k] = jnp.concatenate([half[0, k], half[1, k]], axis=-1)
 
     def upper(k):
-        return full_first[k, :feat]
+        return full_first[k, :, :feat]
 
     def lower(k):
-        return full_first[k, feat:]
+        return full_first[k, :, feat:]
 
     def finish(k, summed):
         half = 0.5 * summed
         hidden = (half + half * jnp.tanh(half)).astype(BF16)
-        result = dot(hidden, full_second[k])
+        result = dot_t(hidden, full_second[k])
         centre = jnp.mean(result, axis=-1, keepdims=True)
         shifted = result - centre
         variance = jnp.mean(shifted * shifted, axis=-1, keepdims=True)
@@ -234,11 +253,11 @@
     node_ids = lax.broadcasted_iota(jnp.int32, (n_enc_rows, n_enc), 0)
     scatter = ones_where(node_ids == kept_row)
     take_weights(0)
-    grid_term = dot(sending, upper(0)) + bias(0)
+    grid_term = dot_t(sending, upper(0)) + bias(0)
     for copy in halo_copies:
         copy.wait_recv()
     target_rows = dot(target_onehot, enc_table[...]).astype(BF16)
-    messages = finish(0, grid_term + dot(target_rows, lower(0))).astype(BF16)
+    messages = finish(0, grid_term + dot_t(target_rows, lower(0))).astype(BF16)
     partial = dot(scatter, messages)
     sum_send[...] = partial[own:].astype(BF16)
     sum_copies = exchange(
@@ -249,35 +268,43 @@
     )
 
     take_weights(1)
-    node_term = dot(block, upper(1)) + bias(1)
+    node_term = dot_t(block, upper(1)) + bias(1)
     take_weights(2)
     take_weights(3)
     for copy in sum_copies:
         copy.wait_recv()
     encode_sum = partial[:own] + dot(enc_unpack_ref[...], sum_recv[...])
-    node_pre = node_term + dot(encode_sum.astype(BF16), lower(1))
+    node_pre = node_term + dot_t(encode_sum.astype(BF16), lower(1))
     mesh_one = (block.astype(F32) + finish(1, node_pre)).astype(BF16)
     mid_table[0] = mesh_one
-    mid_copies = exchange(2, lambda d: mid_table.at[0], lambda d: mid_table.at[1 + d])
+    mid_copies = exchange(
+        2, lambda d: mid_table.at[0], lambda d: mid_table.at[1 + d], 1, (0, 1, 2, 3)
+    )
 
     receiver_row = receiver_ref[...]
     n_edges = receiver_row.shape[1]
     taking_rows = dot(onehot_columns(columns_of(receiver_row), own), mesh_one).astype(BF16)
-    edge_term = dot(taking_rows, lower(2)) + bias(2)
+    edge_term = dot_t(taking_rows, lower(2)) + bias(2)
+    for d in range(2):
+        mid_copies[d].wait_recv()
+        corners = (4 + 2 * d, 5 + 2 * d)
+        mid_copies = mid_copies + exchange(
+            2, lambda c: mid_table.at[1 + d], lambda c: mid_table.at[1 + c], 1, corners
+        )
     own_ids = lax.broadcasted_iota(jnp.int32, (own, n_edges), 0)
     edge_scatter = ones_where(own_ids == receiver_row)
     sender_row = region_index(sender_ref[...], side, side, mid_starts)
     sender_onehot = onehot_columns(columns_of(sender_row), 9 * own)
-    node_term_two = dot(mesh_one, upper(3)) + bias(3)
+    node_term_two = dot_t(mesh_one, upper(3)) + bias(3)
     take_weights(4)
-    grid_taking = dot(grid, lower(4)) + bias(4)
+    grid_taking = dot_t(grid, lower(4)) + bias(4)
     n_dec_rows = own + sum(dec_sizes)
-    for copy in mid_copies:
+    for copy in mid_copies[2:]:
         copy.wait_recv()
     sending_rows = dot(sender_onehot, mid_table[...].reshape(9 * own, feat)).astype(BF16)
-    edge_messages = finish(2, edge_term + dot(sending_rows, upper(2))).astype(BF16)
+    edge_messages = finish(2, edge_term + dot_t(sending_rows, upper(2))).astype(BF16)
     mesh_sum = dot(edge_scatter, edge_messages)
-    node_pre_two = node_term_two + dot(mesh_sum.astype(BF16), lower(3))
+    node_pre_two = node_term_two + dot_t(mesh_sum.astype(BF16), lower(3))
     mesh_two = (mesh_one.astype(F32) + finish(3, node_pre_two)).astype(BF16)
     mesh_out_ref[...] = mesh_two
     dec_send[...] = dot(dec_pack_ref[...], mesh_two).astype(BF16)
@@ -288,10 +315,11 @@
         lambda d: dec_table.at[pl.ds(own + dec_starts[d], dec_sizes[d])],
     )
 
-    dec_rows = region_index(dec_source_ref[...], side, DEC_REACH, dec_starts)
-    dec_ids = lax.broadcasted_iota(jnp.int32, (n_grid, n_dec_rows), 1)
     dec_onehots = [
-        ones_where(dec_rows[:, k : k + 1] == dec_ids) for k in range(dec_rows.shape[1])
+        onehot_columns(
+            columns_of(region_index(dec_source_ref[k], side, DEC_REACH, dec_starts)), n_dec_rows
+        )
+        for k in range(dec_source_ref.shape[0])
     ]
     for copy in dec_copies:
         copy.wait_recv()
@@ -300,7 +328,7 @@
     decode_sum = None
     for onehot in dec_onehots:
         giving_rows = dot(onehot, table).astype(BF16)
-        message = finish(4, grid_taking + dot(giving_rows, upper(4))).astype(BF16).astype(F32)
+        message = finish(4, grid_taking + dot_t(giving_rows, upper(4))).astype(BF16).astype(F32)
         decode_sum = message if decode_sum is None else decode_sum + message
     grid_out_ref[...] = (total + decode_sum).astype(BF16)
 
@@ -327,24 +355,37 @@
     side, _, feat = mesh_latent.shape
     own = side * side
     n_layers = w_first.shape[0]
-    share = w_first.shape[2]
     enc_matrix, _, enc_sizes = packing(side, ENC_REACH)
     dec_matrix, _, dec_sizes = packing(side, DEC_REACH)
     n_enc, n_dec = sum(enc_sizes), sum(dec_sizes)
     vmem = pl.BlockSpec(memory_space=pltpu.VMEM)
     anywhere = pl.BlockSpec(memory_space=pl.ANY)
+    staged = (
+        grid_latent,
+        mesh_latent.reshape(own, feat),
+        first_bias,
+        norm_gain,
+        encode_source.reshape(1, -1),
+        encode_target.reshape(1, -1),
+        encode_count.reshape(1, 1),
+        mesh_sender.reshape(1, -1),
+        mesh_receiver.reshape(1, -1),
+        decode_source.transpose(0, 1, 3, 2).reshape(decode_source.shape[3], 1, -1),
+        jnp.asarray(enc_matrix, BF16),
+        jnp.asarray(enc_matrix.T, BF16),
+        jnp.asarray(dec_matrix, BF16),
+    )
     grid_out, mesh_out = pl.pallas_call(
         functools.partial(kernel, sizes),
         out_shape=(
             jax.ShapeDtypeStruct(grid_latent.shape, BF16),
             jax.ShapeDtypeStruct((own, feat), BF16),
         ),
-        in_specs=[vmem, vmem, anywhere, vmem, anywhere] + [vmem] * 10,
+        in_specs=[anywhere] * (2 + STAGED),
         out_specs=(vmem, vmem),
-        scratch_shapes=[
-            pltpu.VMEM((2, n_layers, 2 * feat, share), BF16),
-            pltpu.VMEM((2, n_layers, feat, share), BF16),
-            pltpu.VMEM((n_layers, 2 * feat, feat), BF16),
+        scratch_shapes=[pltpu.VMEM(array.shape, array.dtype) for array in staged]
+        + [
+            pltpu.VMEM((n_layers, feat, 2 * feat), BF16),
             pltpu.VMEM((n_layers, feat, feat), BF16),
             pltpu.VMEM((n_enc, feat), BF16),
             pltpu.VMEM((own + n_enc, feat), BF16),
@@ -353,6 +394,7 @@
             pltpu.VMEM((9, own, feat), BF16),
             pltpu.VMEM((n_dec, feat), BF16),
             pltpu.VMEM((own + n_dec, feat), BF16),
+            pltpu.SemaphoreType.DMA((STAGED,)),
             pltpu.SemaphoreType.DMA((2, n_layers)),
             pltpu.SemaphoreType.DMA((2, n_layers)),
             pltpu.SemaphoreType.DMA((2, n_layers)),
@@ -360,25 +402,9 @@
             pltpu.SemaphoreType.DMA((4, 8)),
         ],
         compiler_params=pltpu.CompilerParams(
-            collective_id=0, has_side_effects=True, vmem_limit_bytes=48 * 1024 * 1024
+            collective_id=0, has_side_effects=True, vmem_limit_bytes=60 * 1024 * 1024
         ),
-    )(
-        grid_latent,
-        mesh_latent.reshape(own, feat),
-        w_first,
-        first_bias,
-        w_second,
-        norm_gain,
-        encode_source.reshape(1, -1),
-        encode_target.reshape(1, -1),
-        encode_count.reshape(1, 1),
-        mesh_sender.reshape(1, -1),
-        mesh_receiver.reshape(1, -1),
-        decode_source.reshape(decode_source.shape[2:]),
-        jnp.asarray(enc_matrix, BF16),
-        jnp.asarray(enc_matrix.T, BF16),
-        jnp.asarray(dec_matrix, BF16),
-    )
+    )(w_first.transpose(0, 2, 1), w_second.transpose(0, 2, 1), *staged)
     return grid_out, mesh_out.reshape(mesh_latent.shape)
 
 

time: 45 us -> 40.4 us (0.90)
  local copies, waits for them, and re-layouts: 6.69 us -> 3.05 us
  Pallas kernels: 36.6 us -> 35.9 us
    unnamed x27 -> x2, local copies, waits for them, and re-layouts: 6.69 us -> 3.05 us
    pallas_call x1, Pallas kernels: 36.6 us -> 35.9 us  [per_device(): pl.pallas_call(functools.partial(kernel, sizes), out_shape=(jax.ShapeDtyp...]
where the time goes in v2:
time: 40.4 us; the launch traced here: 40.2 us
  Pallas kernels  35.9 us (89%)
  local copies, waits for them, and re-layouts  3.05 us (8%)
  between operations  1.29 us (3%)
    pallas_call x1, Pallas kernels, per_device(): pl.pallas_call(functools.partial(kernel, sizes), out_shape=(jax.ShapeDtyp...  35.9 us
    unnamed x2, local copies, waits for them, and re-layouts  3.05 us

profile of v2, /device:TPU:0, one launch (start us, length us, event | category | flops | bytes accessed | tf_op | source)
XLA Modules:
  0.0 40.2 jit_solution(8600886531897577517)
XLA Ops:
  1.3 35.9 %shard_map.158 = (bf16[256,384]{1,0:T(8,128)(2,1)}, bf16[64,384]{1,0:T(8,128)(2,1)}) custom-call(bf16[5,192,768]{2,1,0:T(8,128)(2,1)} %bitcast.13, bf16[5,192,384]{2,1,0:T(8,128)(2,1)} %bitcast.14, bf16[256,384]{1,0:T(8,128)(2,1)} %refs_2_.1, bf16[64,384]{1,0:T(8,128)(2,1)} %bitcast.16, f32[5,384]{1,0:T(8,128)} %refs_4_.1, f32[5,384]{1,0:T(8,128)} %refs_5_.1, ...), custom_call_target="tpu_custom_call" | custom-call | tf_op jit(solution)/shard_map/pallas_call | solution.py:378
  37.2 1.6 %copy.21 = bf16[256,384]{1,0:T(8,128)(2,1)} copy(bf16[256,384]{1,0:T(8,128)(2,1)} %get-tuple-element.8) | data formatting | bytes 393216
  38.8 1.4 %copy.22 = bf16[8,8,384]{2,1,0:T(8,128)(2,1)} copy(bf16[8,8,384]{2,1,0:T(8,128)(2,1)} %bitcast.15) | data formatting | bytes 98304

commit v3 on v2

--- a/solution.py
+++ b/solution.py
@@ -178,7 +178,7 @@
 
     def exchange(phase, source_of, target_of, towards=1, chosen=None):
         copies = []
-        for d in range(len(DIRS)) if chosen is None else chosen:
+        for d in (0, 1, 4, 5, 6, 7, 2, 3) if chosen is None else chosen:
             dp, dc = DIRS[d][0], DIRS[d][1]
             if chosen and len(chosen) < 4:
                 dp = 0
@@ -378,8 +378,8 @@
     grid_out, mesh_out = pl.pallas_call(
         functools.partial(kernel, sizes),
         out_shape=(
-            jax.ShapeDtypeStruct(grid_latent.shape, BF16),
-            jax.ShapeDtypeStruct((own, feat), BF16),
+            pltpu.VMEM(grid_latent.shape, BF16),
+            pltpu.VMEM((own, feat), BF16),
         ),
         in_specs=[anywhere] * (2 + STAGED),
         out_specs=(vmem, vmem),
@@ -402,7 +402,7 @@
             pltpu.SemaphoreType.DMA((4, 8)),
         ],
         compiler_params=pltpu.CompilerParams(
-            collective_id=0, has_side_effects=True, vmem_limit_bytes=60 * 1024 * 1024
+            collective_id=0, has_side_effects=True, vmem_limit_bytes=56 * 1024 * 1024
         ),
     )(w_first.transpose(0, 2, 1), w_second.transpose(0, 2, 1), *staged)
     return grid_out, mesh_out.reshape(mesh_latent.shape)

time: 40.4 us -> 37.9 us (0.938)
  local copies, waits for them, and re-layouts: 3.05 us -> 1.3 us
  Pallas kernels: 35.9 us -> 35.2 us
    unnamed x2, local copies, waits for them, and re-layouts: 3.05 us -> 1.3 us
    pallas_call x1, Pallas kernels: 35.9 us -> 35.2 us  [per_device(): pl.pallas_call(functools.partial(kernel, sizes), out_shape=(pltpu.VMEM(gr...]
where the time goes in v3:
time: 37.9 us; the launch traced here: 37.8 us
  Pallas kernels  35.2 us (93%)
  local copies, waits for them, and re-layouts  1.3 us (3%)
  between operations  1.29 us (3%)
    pallas_call x1, Pallas kernels, per_device(): pl.pallas_call(functools.partial(kernel, sizes), out_shape=(pltpu.VMEM(gr...  35.2 us
    unnamed x2, local copies, waits for them, and re-layouts  1.3 us

profile of v3, /device:TPU:0, one launch (start us, length us, event | category | flops | bytes accessed | tf_op | source)
XLA Modules:
  0.0 37.8 jit_solution(8494274995545107456)
XLA Ops:
  1.3 35.2 %shard_map.158 = (bf16[256,384]{1,0:T(8,128)(2,1)S(1)}, bf16[64,384]{1,0:T(8,128)(2,1)S(1)}) custom-call(bf16[5,192,768]{2,1,0:T(8,128)(2,1)} %bitcast.14, bf16[5,192,384]{2,1,0:T(8,128)(2,1)} %bitcast.15, bf16[256,384]{1,0:T(8,128)(2,1)} %refs_2_.1, bf16[64,384]{1,0:T(8,128)(2,1)} %bitcast.16, f32[5,384]{1,0:T(8,128)} %refs_4_.1, f32[5,384]{1,0:T(8,128)} %refs_5_.1, ...), custom_call_target="tpu_custom_call" | custom-call | tf_op jit(solution)/shard_map/pallas_call | solution.py:378
  36.5 0.7 %copy.20 = bf16[256,384]{1,0:T(8,128)(2,1)} copy(bf16[256,384]{1,0:T(8,128)(2,1)S(1)} %get-tuple-element.6) | data formatting | bytes 393216
  37.2 0.6 %copy.21 = bf16[8,8,384]{2,1,0:T(8,128)(2,1)} copy(bf16[8,8,384]{2,1,0:T(8,128)(2,1)S(1)} %bitcast.13) | data formatting | bytes 98304

commit v4 on v3

--- a/solution.py
+++ b/solution.py
@@ -258,14 +258,15 @@
         copy.wait_recv()
     target_rows = dot(target_onehot, enc_table[...]).astype(BF16)
     messages = finish(0, grid_term + dot_t(target_rows, lower(0))).astype(BF16)
-    partial = dot(scatter, messages)
-    sum_send[...] = partial[own:].astype(BF16)
+    sum_send[...] = dot(scatter[own:], messages).astype(BF16)
     sum_copies = exchange(
         1,
         lambda d: sum_send.at[pl.ds(enc_starts[d], enc_sizes[d])],
         lambda d: sum_recv.at[pl.ds(enc_starts[d], enc_sizes[d])],
         -1,
     )
+
+    own_partial = dot(scatter[:own], messages)
 
     take_weights(1)
     node_term = dot_t(block, upper(1)) + bias(1)
@@ -273,7 +274,7 @@
     take_weights(3)
     for copy in sum_copies:
         copy.wait_recv()
-    encode_sum = partial[:own] + dot(enc_unpack_ref[...], sum_recv[...])
+    encode_sum = own_partial + dot(enc_unpack_ref[...], sum_recv[...])
     node_pre = node_term + dot_t(encode_sum.astype(BF16), lower(1))
     mesh_one = (block.astype(F32) + finish(1, node_pre)).astype(BF16)
     mid_table[0] = mesh_one
@@ -294,14 +295,22 @@
     own_ids = lax.broadcasted_iota(jnp.int32, (own, n_edges), 0)
     edge_scatter = ones_where(own_ids == receiver_row)
     sender_row = region_index(sender_ref[...], side, side, mid_starts)
-    sender_onehot = onehot_columns(columns_of(sender_row), 9 * own)
+    sender_cols = columns_of(sender_row)
+    sender_near = onehot_columns(sender_cols, 5 * own)
+    sender_far = onehot_columns(sender_cols - 5 * own, 4 * own)
     node_term_two = dot_t(mesh_one, upper(3)) + bias(3)
     take_weights(4)
     grid_taking = dot_t(grid, lower(4)) + bias(4)
     n_dec_rows = own + sum(dec_sizes)
-    for copy in mid_copies[2:]:
+    for copy in mid_copies[2:4]:
         copy.wait_recv()
-    sending_rows = dot(sender_onehot, mid_table[...].reshape(9 * own, feat)).astype(BF16)
+    sending_rows = dot(sender_near, mid_table[:5].reshape(5 * own, feat))
+    for copy in mid_copies[4:]:
+        copy.wait_recv()
+    sending_rows = sending_rows + dot(
+        sender_far, mid_table[5:].reshape(4 * own, feat)
+    )
+    sending_rows = sending_rows.astype(BF16)
     edge_messages = finish(2, edge_term + dot_t(sending_rows, upper(2))).astype(BF16)
     mesh_sum = dot(edge_scatter, edge_messages)
     node_pre_two = node_term_two + dot_t(mesh_sum.astype(BF16), lower(3))
@@ -325,11 +334,11 @@
         copy.wait_recv()
     table = dec_table[...]
     total = grid.astype(F32)
-    decode_sum = None
-    for onehot in dec_onehots:
-        giving_rows = dot(onehot, table).astype(BF16)
-        message = finish(4, grid_taking + dot_t(giving_rows, upper(4))).astype(BF16).astype(F32)
-        decode_sum = message if decode_sum is None else decode_sum + message
+    degree = len(dec_onehots)
+    giving_rows = dot(jnp.concatenate(dec_onehots, axis=0), table).astype(BF16)
+    taking = jnp.concatenate([grid_taking] * degree, axis=0)
+    messages = finish(4, taking + dot_t(giving_rows, upper(4))).astype(BF16).astype(F32)
+    decode_sum = jnp.sum(messages.reshape(degree, n_grid, feat), axis=0)
     grid_out_ref[...] = (total + decode_sum).astype(BF16)
 
     for copies in remote + [halo_copies, sum_copies, mid_copies, dec_copies]:

time: 37.9 us -> 37.7 us (level)
  no operation moved by 1% of the time
where the time goes in v4:
time: 37.7 us; the launch traced here: 37.6 us
  Pallas kernels  35 us (93%)
  local copies, waits for them, and re-layouts  1.3 us (3%)
  between operations  1.29 us (3%)
    pallas_call x1, Pallas kernels, per_device(): pl.pallas_call(functools.partial(kernel, sizes), out_shape=(pltpu.VMEM(gr...  35 us
    unnamed x2, local copies, waits for them, and re-layouts  1.3 us

profile of v4, /device:TPU:0, one launch (start us, length us, event | category | flops | bytes accessed | tf_op | source)
XLA Modules:
  0.0 37.6 jit_solution(5121532838466015418)
XLA Ops:
  1.3 35.0 %shard_map.158 = (bf16[256,384]{1,0:T(8,128)(2,1)S(1)}, bf16[64,384]{1,0:T(8,128)(2,1)S(1)}) custom-call(bf16[5,192,768]{2,1,0:T(8,128)(2,1)} %bitcast.14, bf16[5,192,384]{2,1,0:T(8,128)(2,1)} %bitcast.15, bf16[256,384]{1,0:T(8,128)(2,1)} %refs_2_.1, bf16[64,384]{1,0:T(8,128)(2,1)} %bitcast.16, f32[5,384]{1,0:T(8,128)} %refs_4_.1, f32[5,384]{1,0:T(8,128)} %refs_5_.1, ...), custom_call_target="tpu_custom_call" | custom-call | tf_op jit(solution)/shard_map/pallas_call | solution.py:387
  36.3 0.7 %copy.20 = bf16[256,384]{1,0:T(8,128)(2,1)} copy(bf16[256,384]{1,0:T(8,128)(2,1)S(1)} %get-tuple-element.6) | data formatting | bytes 393216
  37.0 0.6 %copy.21 = bf16[8,8,384]{2,1,0:T(8,128)(2,1)} copy(bf16[8,8,384]{2,1,0:T(8,128)(2,1)S(1)} %bitcast.13) | data formatting | bytes 98304
